TPU v7x, 32 devices: a whole 2x2x4 slice. The times are simulated.
32 devices in a mesh: rep: 2 (over y), pool: 4 (over x, core), tp: 4 (over z).
Axes of the slice: x: 2, y: 2, z: 4, core: 2. Of those that a mesh axis runs over, the one named last changes fastest.
Arguments:
- prompt_states: bfloat16 [12288, 16384], P(('rep', 'pool'), 'tp'), parts along dimension 0, may hold values from -6 to 6
- kv_weight: bfloat16 [16384, 2048], P('tp'), may hold values from -0.046875 to 0.046875
- prompt_lens: int32 [8, 12], P(('rep', 'pool')), parts along dimension 0, may hold values from 1 to 128, 1152 in all within a row
- placement: int32 [96, 1], P(('rep', 'pool')), parts along dimension 0, may hold values from 0 to 3; in each aligned block of 12 rows (0 to 11, 12 to 23, ...) at most 6 rows name the same one
- old_cache: bfloat16 [128, 192, 2048], P(('rep', 'pool'), None, 'tp'), parts along dimension 0, may hold values from -4 to 4
- old_lens: int32 [8, 16], P(('rep', 'pool')), parts along dimension 0, may hold values from 1 to 192, 1536 in all within a row
- query_old: bfloat16 [4, 128, 16384], P(None, ('rep', 'pool'), 'tp'), parts along dimension 1, may hold values from -120 to 120
- step_old: bfloat16 [4, 128, 2048], P(None, ('rep', 'pool'), 'tp'), parts along dimension 1, may hold values from -4 to 4
- query_new: bfloat16 [4, 192, 16384], P(None, ('rep', 'pool'), 'tp'), parts along dimension 1, may hold values from -120 to 120
- step_new: bfloat16 [4, 192, 2048], P(None, ('rep', 'pool'), 'tp'), parts along dimension 1, may hold values from -4 to 4
Outputs:
- attn_old: bfloat16 [4, 128, 16384], P(None, ('rep', 'pool'), 'tp'), parts along dimension 1
- attn_new: bfloat16 [4, 192, 16384], P(None, ('rep', 'pool'), 'tp'), parts along dimension 1
There are 2 independent parts, one for each index of `rep`. A program takes and returns all parts, laid end to end along the dimension named above; an argument that names none is the same for every part. Nothing has to cross between parts.
Inputs may be any that keep to these rules, and one draw needn't show every extreme that they name: `placement`: at most 6 of the 12 prompts of one pool index name the same decode index, and this is reached.
All inputs are finite; a program needn't handle non-finite values.
Results may differ from a plain program's by a relative error of at most 0.019.
Values may be sent and summed in bfloat16 or wider, within the bound.
A program may use at most 128 MiB of HBM per device.

v0:
```python
import math

import jax
import jax.numpy as jnp
from jax import lax
from jax.sharding import PartitionSpec as P

HD = 128


def rotate(vec, pos):
    size = vec.shape[-1]
    half = size // 2
    idx = jnp.arange(half, dtype=jnp.float32)
    freq = jnp.exp(-(2.0 * idx / size) * math.log(500000.0))
    angle = pos[..., None].astype(jnp.float32) * freq
    cosine = jnp.cos(angle)
    sine = jnp.sin(angle)
    first = vec[..., :half]
    second = vec[..., half:]
    return jnp.concatenate(
        [first * cosine - second * sine, second * cosine + first * sine], axis=-1
    )


def decode(query, cache_k, cache_v, lens, step_kv):
    steps, count = (query.shape[0], query.shape[1])
    heads, width = (cache_k.shape[2], cache_k.shape[3])
    group = query.shape[2] // (heads * width)
    pos = lens[None, :] + jnp.arange(steps, dtype=jnp.int32)[:, None]
    q_rot = rotate(
        query.reshape(steps, count, heads, group, width).astype(jnp.float32), pos[:, :, None, None]
    ).astype(jnp.bfloat16)
    pairs = step_kv.reshape(steps, count, heads, 2, width)
    s_key = rotate(pairs[:, :, :, 0].astype(jnp.float32), pos[:, :, None]).astype(jnp.bfloat16)
    s_val = pairs[:, :, :, 1]
    scale = 1.0 / math.sqrt(width)
    sc_cache = (
        jnp.einsum("sbhqd,blhd->sbhql", q_rot, cache_k, preferred_element_type=jnp.float32) * scale
    )
    sc_step = (
        jnp.einsum("sbhqd,tbhd->sbhqt", q_rot, s_key, preferred_element_type=jnp.float32) * scale
    )
    rows = cache_k.shape[1]
    mask_cache = (jnp.arange(rows, dtype=jnp.int32)[None, :] < lens[:, None])[
        None, :, None, None, :
    ]
    mask_step = (
        jnp.arange(steps, dtype=jnp.int32)[None, :] <= jnp.arange(steps, dtype=jnp.int32)[:, None]
    )[:, None, None, None, :]
    low = jnp.float32(-1e30)
    sc_cache = jnp.where(mask_cache, sc_cache, low)
    sc_step = jnp.where(mask_step, sc_step, low)
    top = jnp.maximum(jnp.max(sc_cache, axis=-1), jnp.max(sc_step, axis=-1))[..., None]
    ex_cache = jnp.where(mask_cache, jnp.exp(sc_cache - top), 0.0)
    ex_step = jnp.where(mask_step, jnp.exp(sc_step - top), 0.0)
    total = jnp.sum(ex_cache, axis=-1, keepdims=True) + jnp.sum(ex_step, axis=-1, keepdims=True)
    w_cache = (ex_cache / total).astype(jnp.bfloat16)
    w_step = (ex_step / total).astype(jnp.bfloat16)
    out = jnp.einsum("sbhql,blhd->sbhqd", w_cache, cache_v, preferred_element_type=jnp.float32)
    out = out + jnp.einsum("sbhqt,tbhd->sbhqd", w_step, s_val, preferred_element_type=jnp.float32)
    return out.reshape(steps, count, heads * group * width).astype(jnp.bfloat16)


def local(
    prompt_states,
    kv_weight,
    prompt_lens,
    placement,
    old_cache,
    old_lens,
    query_old,
    step_old,
    query_new,
    step_new,
):
    tok_rows = prompt_states.shape[0]
    columns = kv_weight.shape[1]
    tp_size = lax.axis_size("tp")
    pool_size = lax.axis_size("pool")
    local_prompts = prompt_lens.shape[1]
    plen = tok_rows // local_prompts
    capacity = max(2, 2 * local_prompts // pool_size)
    width = HD
    local_heads = columns // tp_size // (2 * width)
    kv_cols = lax.psum_scatter(
        lax.dot_general(
            kv_weight, prompt_states, (((0,), (1,)), ((), ())), preferred_element_type=jnp.float32
        ).astype(jnp.bfloat16),
        "tp",
        scatter_dimension=0,
        tiled=True,
    ).astype(jnp.float32)
    kv_proj = kv_cols.T.reshape(tok_rows, local_heads, 2, width)
    position = jnp.arange(tok_rows, dtype=jnp.int32) % plen
    keys = rotate(kv_proj[:, :, 0], position[:, None]).astype(jnp.bfloat16)
    values = kv_proj[:, :, 1].astype(jnp.bfloat16)
    flat_cache = jnp.stack([keys, values], axis=2).reshape(
        local_prompts, plen * local_heads * 2 * width
    )
    dest = placement[:, 0]
    onehot = (dest[:, None] == jnp.arange(pool_size, dtype=jnp.int32)[None, :]).astype(jnp.int32)
    before = jnp.cumsum(onehot, axis=0) - onehot
    rank = jnp.sum(before * onehot, axis=1)
    lengths = prompt_lens[0]
    slots = pool_size * capacity
    here = lax.axis_index("pool")
    p_cache = lax.all_gather(flat_cache, "pool", axis=0, tiled=True)
    p_dest = lax.all_gather(dest, "pool", axis=0, tiled=True)
    p_rank = lax.all_gather(rank, "pool", axis=0, tiled=True)
    p_lens = lax.all_gather(lengths, "pool", axis=0, tiled=True)
    count = p_cache.shape[0]
    source = jnp.arange(count, dtype=jnp.int32) // local_prompts
    target = source * capacity + p_rank
    picked = (p_dest[:, None] == here) & (
        target[:, None] == jnp.arange(slots, dtype=jnp.int32)[None, :]
    )
    moved = jnp.einsum(
        "js,jf->sf", picked.astype(jnp.bfloat16), p_cache, preferred_element_type=jnp.float32
    )
    stored = moved.astype(jnp.bfloat16)
    lens_now = jnp.sum(jnp.where(picked, p_lens[:, None], 0), axis=0).astype(jnp.int32)
    new_cache = stored.reshape(slots, plen, local_heads, 2, width)
    resident = old_cache.reshape(old_cache.shape[0], old_cache.shape[1], local_heads, 2, width)
    attn_old = decode(query_old, resident[:, :, :, 0], resident[:, :, :, 1], old_lens[0], step_old)
    attn_new = decode(query_new, new_cache[:, :, :, 0], new_cache[:, :, :, 1], lens_now, step_new)
    return (attn_old, attn_new)


def solution(mesh):
    return jax.shard_map(
        local,
        mesh=mesh,
        in_specs=(
            P(("rep", "pool"), "tp"),
            P("tp", None),
            P(("rep", "pool"), None),
            P(("rep", "pool"), None),
            P(("rep", "pool"), None, "tp"),
            P(("rep", "pool"), None),
            P(None, ("rep", "pool"), "tp"),
            P(None, ("rep", "pool"), "tp"),
            P(None, ("rep", "pool"), "tp"),
            P(None, ("rep", "pool"), "tp"),
        ),
        out_specs=(P(None, ("rep", "pool"), "tp"), P(None, ("rep", "pool"), "tp")),
        check_vma=False,
    )
```

profile of v0, /device:TPU:12, one launch (start us, length us, event | category | flops | bytes accessed | tf_op | source)
XLA Modules:
  0.0 251.1 jit_solution(6831333362628824236)
XLA Ops:
  7.2 0.0 reduce-scatter.2.cloned.1.call-start
  7.2 33.9 %convolution_convert_fusion.1 = bf16[2048,1536]{1,0:T(8,128)(2,1)} fusion(bf16[4096,2048]{1,0:T(8,128)(2,1)} %param.11, bf16[1536,4096]{1,0:T(8,128)(2,1)} %param.10), kind=kOutput, calls=%fused_computation.1 | convolution fusion | flops 25772949504 | bytes 35651584 | tf_op jit(solution)/shard_map/dot_general | solution.py:87
  41.2 0.0 reduce-scatter.2.cloned.1.call-update
  41.2 0.2 all-gather.5.cloned.1.call-start
  41.4 1.4 multiply_cosine_fusion
  42.9 110.3 %reduce-scatter.2.cloned.1.call-done = bf16[512,1536]{1,0:T(8,128)(2,1)} async-done(((bf16[2048,1536]{1,0:T(8,128)(2,1)}), bf16[512,1536]{1,0:T(8,128)(2,1)}) %reduce-scatter.2.cloned.1.call-update) | async-done | bytes 1572880 | tf_op jit(solution)/shard_map/reduce_scatter | solution.py:86
  153.2 1.5 fusion.24
  154.8 0.3 fusion.29
  155.0 0.1 pad_maximum_fusion
  155.1 1.2 copy.73
  156.3 2.4 reshape.379
  158.7 0.0 all-gather.5.cloned.1.call-update
  158.8 1.4 copy.102
  160.2 1.1 copy.101
  161.3 0.0 copy-start.11
  161.3 3.8 %reshape.355 = bf16[16,192,2,2,128]{4,3,2,1,0:T(2,128)(2,1)S(1)} reshape(bf16[16,192,512]{2,1,0:T(8,128)(2,1)} %param.14) | data formatting | bytes 6291456 | tf_op jit(solution)/shard_map/reshape | solution.py:124
  165.1 0.1 iota_compare_fusion
  165.2 0.1 add_convert_fusion.6
  165.3 0.3 multiply_cosine_fusion.2
  165.6 0.1 fusion.74
  165.8 0.1 subtract_convert_fusion.4
  165.9 2.2 fusion.72
  168.1 0.3 subtract_convert_fusion.1
  168.4 1.5 fusion.75
  169.9 5.7 %fusion.70 = (bf16[16,192,2,1,128]{4,3,2,1,0:T(2,128)(2,1)S(1)}, bf16[16,192,2,1,128]{4,3,2,1,0:T(2,128)(2,1)S(1)}) fusion(bf16[16,192,2,2,128]{4,3,2,1,0:T(2,128)(2,1)S(1)} %reshape.355), kind=kLoop, calls=%fused_computation.136 | loop fusion | bytes 6291456 | tf_op jit(solution)/shard_map/slice | solution.py:125
  175.6 1.3 bitcast_reduce_fusion
  177.0 0.3 fusion.37
  177.3 1.1 fusion.9
  178.4 1.4 fusion.4
  179.8 0.0 copy-start.14
  179.8 0.0 copy-start.12
  179.8 0.0 copy-start.13
  179.8 0.5 fusion.12
  180.3 1.0 convert_element_type.127
  181.4 0.6 dynamic-slice
  182.6 0.2 reduce_window_sum.11
  182.8 0.2 dynamic-update-slice.1
  183.1 0.1 bitcast_dynamic-update-slice_fusion.1
  183.2 0.1 bitcast_dynamic-update-slice_fusion
  183.3 4.9 %all-reduce.3 = (s32[48]{0:T(128)S(1)}, s32[48]{0:T(128)S(1)}, s32[48]{0:T(128)S(1)}) all-reduce(s32[48]{0:T(128)S(1)} %bitcast_dynamic-update-slice_fusion, s32[48]{0:T(128)S(1)} %dynamic-update-slice.1, s32[48]{0:T(128)S(1)} %bitcast_dynamic-update-slice_fusion.1), channel_id=3, replica_groups=mesh['rep'=2,'pool'=4,'tp'=4] {'pool'}, use_global_device_ids=true, to_apply=%add.2 | all-reduce | flops 144 | bytes 1152
  188.2 0.1 select_reduce_fusion
  188.3 0.1 iota_compare_fusion.1
  188.4 0.1 add_convert_fusion.5
  188.5 0.4 multiply_cosine_fusion.1
  188.9 0.8 fusion.73
  189.7 0.1 subtract_convert_fusion.3
  189.9 0.6 fusion.71
  190.5 0.5 subtract_convert_fusion
  191.0 0.9 copy-done.1
  191.9 0.2 copy-done.3
  192.1 2.8 %fusion.76 = (f32[4,24,2,16]{3,0,2,1:T(4,128)}, f32[4,24,2,16,4]{3,4,0,2,1:T(4,128)S(1)}) fusion(bf16[4,24,2,16,64]{4,3,0,2,1:T(8,128)(2,1)S(1)} %get-tuple-element.6, bf16[4,24,2,16,64]{4,3,0,2,1:T(8,128)(2,1)S(1)} %get-tuple-element.5, bf16[4,24,2,64]{3,0,2,1:T(4,128)(2,1)S(1)} %get-tuple-element.22, bf16[4,24,2,64]{3,0,2,1:T(4,128)(2,1)S(1)} %get-tuple-element.21, ...), kind=kOutput, calls=%fused_computation.142 | convolution fusion | flops 4850688 | bytes 897040 | tf_op jit(solution)/shard_map/sbhqd,tbhd->sbhqt/dot_general | solution.py:42
  194.9 22.9 %all-gather.5.cloned.1.call-done = bf16[4,12,65536]{2,1,0:T(8,128)(2,1)} async-done(((bf16[1,12,65536]{2,1,0:T(8,128)(2,1)}), bf16[4,12,65536]{2,1,0:T(8,128)(2,1)}) %all-gather.5.cloned.1.call-update) | async-done | bytes 6291472 | tf_op jit(solution)/shard_map/all_gather | solution.py:108
  217.8 6.0 %reshape.380 = bf16[48,65536]{1,0:T(8,128)(2,1)} reshape(bf16[4,12,65536]{2,1,0:T(8,128)(2,1)} %all-gather.5.cloned.1.call-done) | data formatting | bytes 12582912
  223.8 5.4 %convolution_convert_fusion = bf16[24,65536]{1,0:T(8,128)(2,1)} fusion(bf16[48,65536]{1,0:T(8,128)(2,1)} %reshape.380, s32[48]{0:T(128)S(1)} %fusion.58, pred[48]{0:T(512)(128)(4,1)S(1)} %broadcast_compare_fusion), kind=kOutput, calls=%fused_computation | convolution fusion | flops 152570112 | bytes 9437424 | tf_op jit(solution)/shard_map/js,jf->sf/dot_general | solution.py:118
  229.2 4.3 %reshape.359 = bf16[24,128,2,2,128]{4,3,2,1,0:T(2,128)(2,1)S(1)} reshape(bf16[24,65536]{1,0:T(8,128)(2,1)} %convolution_convert_fusion) | data formatting | bytes 6291456 | tf_op jit(solution)/shard_map/reshape | solution.py:123
  233.5 0.0 copy-start.4
  233.5 4.5 %fusion.69 = (bf16[24,128,2,1,128]{4,3,2,1,0:T(2,128)(2,1)S(1)}, bf16[24,128,2,1,128]{4,3,2,1,0:T(2,128)(2,1)S(1)}) fusion(bf16[24,128,2,2,128]{4,3,2,1,0:T(2,128)(2,1)S(1)} %reshape.359), kind=kLoop, calls=%fused_computation.135 | loop fusion | bytes 6291456 | tf_op jit(solution)/shard_map/slice | solution.py:126
  238.0 1.4 bitcast_reduce_fusion.1
  239.4 0.4 fusion.31
  239.8 1.0 fusion.11
  240.9 0.6 fusion.32
  241.5 1.4 fusion.6
  242.9 0.1 copy.80
  243.1 1.2 convert_element_type.140
  (42 shorter events, 0.4 us)
Async XLA Ops:
  7.2 146.0 %reduce-scatter.2.cloned.1.call-start = ((), (), s32[]{:S(2)}) async-start(), calls=%async_computation.1 | async-start | bytes 7864320 | tf_op jit(solution)/shard_map/reduce_scatter | solution.py:86
  41.2 176.6 %all-gather.5.cloned.1.call-start = ((), (), s32[]{:S(2)}) async-start(), calls=%async_computation.2 | async-start | bytes 10485760 | tf_op jit(solution)/shard_map/all_gather | solution.py:108
  156.3 2.5 copy-start.5
  158.7 1.4 copy-start.8
  158.7 1.5 copy-start.6
  158.7 2.6 %copy-start.10 = (bf16[4,16,512]{2,1,0:T(8,128)(2,1)S(1)}, bf16[4,16,512]{2,1,0:T(8,128)(2,1)}, u32[]{:S(2)}) copy-start(bf16[4,16,512]{2,1,0:T(8,128)(2,1)} %param.17) | copy-start | bytes 196612
  161.3 3.8 %copy-start.11 = (s32[1,16]{1,0:T(1,128)S(1)}, s32[1,16]{1,0:T(1,128)}, u32[]{:S(2)}) copy-start(s32[1,16]{1,0:T(1,128)} %param.15) | copy-start | bytes 196
  179.8 1.6 copy-start.14
  179.8 2.8 %copy-start.12 = (s32[12,1]{0,1:T(1,128)S(1)}, s32[12,1]{0,1:T(1,128)}, u32[]{:S(2)}) copy-start(s32[12,1]{0,1:T(1,128)} %param.13) | copy-start | bytes 148
  179.8 3.4 %copy-start.13 = (s32[1,12]{1,0:T(1,128)S(1)}, s32[1,12]{1,0:T(1,128)}, u32[]{:S(2)}) copy-start(s32[1,12]{1,0:T(1,128)} %param.12) | copy-start | bytes 148
  180.3 9.6 %copy-start = (f32[12,8,32,128]{3,2,1,0:T(8,128)S(1)}, f32[12,8,32,128]{3,2,1,0:T(8,128)}, u32[]{:S(2)}) copy-start(f32[12,8,32,128]{3,2,1,0:T(8,128)} %copy.102) | copy-start | bytes 4718596
  191.0 0.9 copy-start.1
  191.0 1.1 copy-start.3
  233.5 4.5 %copy-start.2 = (bf16[4,24,2,16,64]{4,3,0,2,1:T(8,128)(2,1)S(1)}, bf16[4,24,2,16,64]{4,3,0,2,1:T(8,128)(2,1)}, u32[]{:S(2)}) copy-start(bf16[4,24,2,16,64]{4,3,0,2,1:T(8,128)(2,1)} %copy-done.1) | copy-start | bytes 1179652
  233.5 4.5 %copy-start.4 = (bf16[4,24,2,16,64]{4,3,0,2,1:T(8,128)(2,1)S(1)}, bf16[4,24,2,16,64]{4,3,0,2,1:T(8,128)(2,1)}, u32[]{:S(2)}) copy-start(bf16[4,24,2,16,64]{4,3,0,2,1:T(8,128)(2,1)} %copy-done.3) | copy-start | bytes 1179652
  238.0 1.4 copy-start.7
  239.4 1.5 copy-start.9
Sparse Core Ops, SparseCore 0:
  41.3 111.8 reduce-scatter.1
  158.9 58.8 all-gather.4
where the time goes:
time: 253 us; the launch traced here: 251 us
  waiting for transfers between devices  133 us (53%)
  matrix products  50.2 us (20%)
  local copies, waits for them, and re-layouts  38.6 us (15%)
  between operations  15.1 us (6%)
  other arithmetic  8.78 us (3%)
  blocking collectives  4.93 us (2%)
    reduce_scatter x1, waiting for transfers between devices, local(): lax.psum_scatter(lax.dot_general(kv_weight, prompt_states, (((0,), (1,)),...  110 us
    dot_general x1, matrix products, local(): lax.dot_general(kv_weight, prompt_states, (((0,), (1,)), ((), ())), prefe...  33.9 us
    all_gather x1, waiting for transfers between devices, local(): p_cache = lax.all_gather(flat_cache, 'pool', axis=0, tiled=True)  22.9 us
    unnamed x41, local copies, waits for them, and re-layouts  13.1 us
    slice x1, local copies, waits for them, and re-layouts, local(): resident[:, :, :, 0]  5.74 us
    dot_general x1, matrix products, local(): jnp.einsum('js,jf->sf', picked.astype(jnp.bfloat16), p_cache, preferred_e...  5.41 us
  transfers between devices with their start and end apart: 2, of which 2 were waited for; matrix products, arithmetic and copies ran while one was open for 12% of the time, Pallas kernels for 0%

commit v1 on v0

v1 whole, which is shorter than its diff:
```python
import functools
import math

import jax
import jax.numpy as jnp
import numpy as np
from jax import lax
from jax.experimental import pallas as pl
from jax.experimental.pallas import tpu as pltpu
from jax.sharding import PartitionSpec as P

HD = 128
PIECES = 3
MESH = pl.DeviceIdType.MESH
F32 = jnp.float32
BF16 = jnp.bfloat16


def turn(v, cosine, sine):
    return v * cosine + pltpu.roll(v, HD // 2, v.ndim - 1) * sine


def tables(pos):
    half = HD // 2
    freq = jnp.exp(-(2.0 * jnp.arange(half, dtype=F32) / HD) * math.log(500000.0))
    angle = pos[..., None].astype(F32) * freq
    c, s = jnp.cos(angle), jnp.sin(angle)
    return jnp.concatenate([c, c, -s, s], axis=-1)


def kernel(
    dims,
    x, w, target, ptab, q_old, s_old, cache, tab_old, q_new, s_new, tab_new,
    len_old, off_new, len_new,
    o_old, o_new,
    wbuf, y, pick, part, rbuf, qs, ks, vs, os_, store, *rest,
):
    n, pool, heads, group, plen, cap, rows, packed = dims
    pbuf = rest[:heads]
    wsem, zsend, zrecv, agsend, agrecv, fwsend = rest[heads:]
    z, me = lax.axis_index("tp"), lax.axis_index("pool")
    chips = pool // 2
    chip, core = me // 2, lax.rem(me, 2)
    mate = chip * 2 + 1 - core
    size = packed // PIECES
    slack = rows - packed
    steps = q_old.shape[0]

    def peer(k):
        return lax.rem(chip + k, chips) * 2 + core

    def source(k):
        return lax.rem(chip + chips - k, chips) * 2 + core

    def order(k):
        middle = n - 1 - k // 2 if k % 2 == 0 else (k - 1) // 2
        return jnp.where(z == 0, n - 1 - k, jnp.where(z == n - 1, k, middle))

    blocks = [(h, k) for h in range(heads) for k in range(n)]

    def weights(i):
        h, k = blocks[i]
        first = pl.multiple_of((order(k) * heads + h) * 2 * HD, 2 * HD)
        return pltpu.make_async_copy(
            w.at[:, pl.ds(first, 2 * HD)], wbuf.at[i % 2], wsem.at[i % 2]
        )

    weights(0).start()

    barrier = pltpu.get_barrier_semaphore()

    @pl.when(z > 0)
    def _():
        pl.semaphore_signal(barrier, inc=1, device_id={"tp": z - 1}, device_id_type=MESH)

    @pl.when(z < n - 1)
    def _():
        pl.semaphore_signal(barrier, inc=1, device_id={"tp": z + 1}, device_id_type=MESH)

    pl.semaphore_signal(barrier, inc=1, device_id={"pool": mate}, device_id_type=MESH)
    for k in range(1, chips):
        pl.semaphore_signal(barrier, inc=1, device_id={"pool": peer(k)}, device_id_type=MESH)
    for p in range(PIECES):
        wanted = target[:, p * size : (p + 1) * size + slack]
        line = lax.broadcasted_iota(jnp.int32, (size, size + slack), 0) + p * size
        pick[p] = jnp.where(line == wanted, 1.0, 0.0).astype(BF16)
    ks[...] = jnp.zeros_like(ks)
    vs[...] = jnp.zeros_like(vs)
    edges = (z > 0).astype(jnp.int32) + (z < n - 1).astype(jnp.int32)
    pl.semaphore_wait(barrier, edges + chips)

    def span(p):
        return pl.ds(p * size, size)

    def up(d, h, p):
        return pltpu.make_async_remote_copy(
            part.at[d, h, span(p)], rbuf.at[0, d, h, span(p)],
            zsend.at[d, h, p], zrecv.at[0, d, h, p],
            device_id={"tp": z + 1}, device_id_type=MESH,
        )

    def down(d, h, p):
        return pltpu.make_async_remote_copy(
            part.at[d, h, span(p)], rbuf.at[1, d, h, span(p)],
            zsend.at[d, h, p], zrecv.at[1, d, h, p],
            device_id={"tp": z - 1}, device_id_type=MESH,
        )

    def share(h, p, k):
        return pltpu.make_async_remote_copy(
            pbuf[h].at[me, span(p)], pbuf[h].at[me, span(p)],
            agsend.at[k, h, p], agrecv.at[me, h, p],
            device_id={"pool": mate if k == 0 else peer(k)}, device_id_type=MESH,
        )

    def forward(h, p, k):
        src = source(k)
        return pltpu.make_async_remote_copy(
            pbuf[h].at[src, span(p)], pbuf[h].at[src, span(p)],
            fwsend.at[k, h, p], agrecv.at[src, h, p],
            device_id={"pool": mate}, device_id_type=MESH,
        )

    def arrived(h, p, src):
        return pltpu.make_async_remote_copy(
            pbuf[h].at[src, span(p)], pbuf[h].at[src, span(p)],
            fwsend.at[0, h, p], agrecv.at[src, h, p],
            device_id={"pool": mate}, device_id_type=MESH,
        )

    def multiply(i):
        h, k = blocks[i]
        d = order(k)
        if i + 1 < len(blocks):
            weights(i + 1).start()
        weights(i).wait()
        tile = 4 * plen

        def body(r, carry):
            at = pl.ds(pl.multiple_of(r * tile, tile), tile)
            got = jnp.dot(x[at, :], wbuf[i % 2], preferred_element_type=F32)
            y[at, HD:] = got[:, HD:].astype(BF16)
            key = got[:, :HD].reshape(4, plen, HD)
            key = turn(key, ptab[:, :HD][None], ptab[:, HD:][None])
            y[at, :HD] = key.reshape(tile, HD).astype(BF16)
            return carry

        lax.fori_loop(0, rows // tile, body, 0)
        for p in range(PIECES):
            part[d, h, span(p)] = jnp.dot(
                pick[p], y[p * size : (p + 1) * size + slack], preferred_element_type=F32
            ).astype(BF16)

            @pl.when((z == 0) & (d > 0))
            def _():
                up(d, h, p).start()

            @pl.when((z == n - 1) & (d < n - 1))
            def _():
                down(d, h, p).start()

    def relay(h, s):
        for p in range(PIECES):
            high, low = n - 1 - s, s

            @pl.when((z > 0) & (z < high))
            def _():
                up(high, h, p).wait_recv()
                part[high, h, span(p)] = (
                    part[high, h, span(p)].astype(F32) + rbuf[0, high, h, span(p)].astype(F32)
                ).astype(BF16)
                up(high, h, p).start()

            @pl.when((z < n - 1) & (z > low))
            def _():
                down(low, h, p).wait_recv()
                part[low, h, span(p)] = (
                    part[low, h, span(p)].astype(F32) + rbuf[1, low, h, span(p)].astype(F32)
                ).astype(BF16)
                down(low, h, p).start()

            last = jnp.maximum(
                jnp.where(z > 0, n - 1 - z, 0), jnp.where(z < n - 1, z, 0)
            )

            @pl.when(last == s)
            def _():
                mine = pbuf[h].at[me, span(p)]

                @pl.when(z == 0)
                def _():
                    down(z, h, p).wait_recv()
                    mine[...] = (
                        part[z, h, span(p)].astype(F32) + rbuf[1, z, h, span(p)].astype(F32)
                    ).astype(BF16)

                @pl.when(z == n - 1)
                def _():
                    up(z, h, p).wait_recv()
                    mine[...] = (
                        part[z, h, span(p)].astype(F32) + rbuf[0, z, h, span(p)].astype(F32)
                    ).astype(BF16)

                @pl.when((z > 0) & (z < n - 1))
                def _():
                    up(z, h, p).wait_recv()
                    down(z, h, p).wait_recv()
                    mine[...] = (
                        part[z, h, span(p)].astype(F32)
                        + rbuf[0, z, h, span(p)].astype(F32)
                        + rbuf[1, z, h, span(p)].astype(F32)
                    ).astype(BF16)

                for k in range(chips):
                    share(h, p, k).start()

    def spread(h):
        for p in range(PIECES):
            for k in range(1, chips):
                arrived(h, p, source(k)).wait_recv()
                forward(h, p, k).start()

    def collect(h):
        for p in range(PIECES):
            for k in range(chips):
                arrived(h, p, lax.rem(chip + k, chips) * 2 + 1 - core).wait_recv()

    def attend(h, q, st, tab, out, block, width, per, count):
        for t in range(steps):
            c, s = tab[t, :, :HD], tab[t, :, HD:]
            for g in range(group):
                col = (h * group + g) * HD
                at = (t * group + g) * count
                qs[at : at + count, :] = turn(q[t, :, col : col + HD].astype(F32), c, s)
            col = h * 2 * HD
            ks[t * count : (t + 1) * count, :] = turn(st[t, :, col : col + HD].astype(F32), c, s)
            vs[t * count : (t + 1) * count, :] = st[t, :, col + HD : col + 2 * HD].astype(F32)
        if count * steps < ks.shape[0]:
            ks[count * steps :, :] = jnp.zeros((ks.shape[0] - count * steps, HD), F32)
            vs[count * steps :, :] = jnp.zeros((ks.shape[0] - count * steps, HD), F32)
        m = steps * group
        col = lax.broadcasted_iota(jnp.int32, (m, width + 16), 1)
        now = lax.broadcasted_iota(jnp.int32, (m, width + 16), 0) // group
        recent = (col >= width) & (col - width <= now)

        def body(i, carry):
            for j in range(per):
                b = i * per + j
                kv, low, high = block(b, h)
                query = qs[pl.ds(b, m, stride=count), :].astype(BF16)
                own_k = ks[pl.ds(b, 16, stride=count), :].astype(BF16)
                own_v = vs[pl.ds(b, 16, stride=count), :].astype(BF16)
                keys = jnp.concatenate([kv[:, :HD], own_k], axis=0)
                values = jnp.concatenate([kv[:, HD:], own_v], axis=0)
                score = lax.dot_general(
                    query, keys, (((1,), (1,)), ((), ())), preferred_element_type=F32
                ) * (1.0 / math.sqrt(HD))
                keep = ((col >= low) & (col < high)) | recent
                score = jnp.where(keep, score, -1e30)
                top = jnp.max(score, axis=-1, keepdims=True)
                e = jnp.where(keep, jnp.exp(score - top), 0.0)
                total = jnp.sum(e, axis=-1, keepdims=True)
                got = jnp.dot((e / total).astype(BF16), values, preferred_element_type=F32)
                os_[pl.ds(b, m, stride=count), :] = got
            return carry

        lax.fori_loop(0, count // per, body, 0)
        for t in range(steps):
            for g in range(group):
                c0 = (h * group + g) * HD
                at = (t * group + g) * count
                out[t, :, c0 : c0 + HD] = os_[at : at + count, :].astype(BF16)

    def resident(b, h):
        return cache[b, :, h * 2 * HD : (h + 1) * 2 * HD], 0, len_old[b]

    def placed(b, h):
        return store[b], 0, len_new[b]

    def place(h):
        ahead = lax.broadcasted_iota(jnp.int32, (plen, packed), 1) - lax.broadcasted_iota(
            jnp.int32, (plen, packed), 0
        )

        def body(s, carry):
            got = pbuf[h][s]
            chosen = jnp.concatenate(
                [
                    jnp.where(ahead == off_new[s * cap + j], 1.0, 0.0).astype(BF16)
                    for j in range(cap)
                ],
                axis=0,
            )
            rows_of = jnp.dot(chosen, got, preferred_element_type=F32).astype(BF16)
            for j in range(cap):
                store[s * cap + j] = rows_of[j * plen : (j + 1) * plen]
            return carry

        lax.fori_loop(0, pool, body, 0)

    def old(h):
        attend(h, q_old, s_old, tab_old, o_old, resident, cache.shape[1], 4, q_old.shape[1])

    def new(h):
        collect(h)
        place(h)
        attend(h, q_new, s_new, tab_new, o_new, placed, plen, 4, q_new.shape[1])

    for i in range(n):
        multiply(i)
    later = []
    for h in range(heads):
        ahead = list(range((h + 1) * n, (h + 2) * n)) if h + 1 < heads else []
        for s in range(n - 1):
            relay(h, s)
            if ahead:
                multiply(ahead.pop(0))
            elif later:
                later.pop(0)()
        for i in ahead:
            multiply(i)
        spread(h)
        if h == 0:
            for g in range(heads):
                later.append(functools.partial(old, g))
            if heads > 1:
                later.pop(0)()
        later.append(functools.partial(new, h))
    for f in later:
        f()

    for h in range(heads):
        for p in range(PIECES):
            for d in range(n):

                @pl.when(z < d)
                def _():
                    up(d, h, p).wait_send()

                @pl.when(z > d)
                def _():
                    down(d, h, p).wait_send()

            for k in range(chips):
                share(h, p, k).wait_send()
            for k in range(1, chips):
                forward(h, p, k).wait_send()


def local(
    prompt_states,
    kv_weight,
    prompt_lens,
    placement,
    old_cache,
    old_lens,
    query_old,
    step_old,
    query_new,
    step_new,
):
    rows = prompt_states.shape[0]
    n, pool = lax.axis_size("tp"), lax.axis_size("pool")
    prompts = prompt_lens.shape[1]
    plen = rows // prompts
    packed = rows * 3 // 4
    heads = kv_weight.shape[1] // n // (2 * HD)
    group = query_old.shape[2] // (heads * HD)
    steps, olds = query_old.shape[:2]
    slots = query_new.shape[1]
    cap = slots // pool

    lens = prompt_lens[0]
    begin = jnp.cumsum(lens) - lens
    k = jnp.arange(plen, dtype=jnp.int32)[None]
    target = jnp.where(k < lens[:, None], begin[:, None] + k, -1).reshape(1, rows)

    meta = lax.all_gather(jnp.stack([lens, placement[:, 0]]), "pool")
    all_lens, dest = meta[:, 0], meta[:, 1]
    all_begin = jnp.cumsum(all_lens, axis=1) - all_lens
    here = (dest == lax.axis_index("pool")).astype(jnp.int32)
    rank = jnp.cumsum(here, axis=1) - here
    hit = (here[:, None, :] > 0) & (
        rank[:, None, :] == jnp.arange(cap, dtype=jnp.int32)[None, :, None]
    )
    len_new = jnp.sum(jnp.where(hit, all_lens[:, None], 0), axis=2).reshape(slots)
    off_new = jnp.sum(jnp.where(hit, all_begin[:, None], 0), axis=2).reshape(slots)
    t = jnp.arange(steps, dtype=jnp.int32)[:, None]
    tab_old = tables(old_lens + t)
    tab_new = tables(len_new[None] + t)
    half = HD // 2
    angle = np.arange(plen, dtype=np.float32)[:, None] * np.exp(
        -(2.0 * np.arange(half, dtype=np.float32) / HD) * np.float32(math.log(500000.0))
    ).astype(np.float32)
    c, s = np.cos(angle), np.sin(angle)
    ptab = jnp.asarray(np.concatenate([c, c, -s, s], axis=1).astype(np.float32))

    vmem = pl.BlockSpec(memory_space=pltpu.VMEM)
    smem = pl.BlockSpec(memory_space=pltpu.SMEM)
    most = max(olds, slots)
    m = steps * group
    dims = (n, pool, heads, group, plen, cap, rows, packed)
    dma = pltpu.SemaphoreType.DMA
    size = packed // PIECES
    return pl.pallas_call(
        functools.partial(kernel, dims),
        out_shape=(
            jax.ShapeDtypeStruct(query_old.shape, BF16),
            jax.ShapeDtypeStruct(query_new.shape, BF16),
        ),
        in_specs=[vmem, pl.BlockSpec(memory_space=pl.ANY)] + [vmem] * 9 + [smem] * 3,
        out_specs=(vmem, vmem),
        scratch_shapes=[
            pltpu.VMEM((2, kv_weight.shape[0], 2 * HD), BF16),
            pltpu.VMEM((rows, 2 * HD), BF16),
            pltpu.VMEM((PIECES, size, size + rows - packed), BF16),
            pltpu.VMEM((n, heads, packed, 2 * HD), BF16),
            pltpu.VMEM((2, n, heads, packed, 2 * HD), BF16),
            pltpu.VMEM((m * most, HD), F32),
            pltpu.VMEM((16 * most, HD), F32),
            pltpu.VMEM((16 * most, HD), F32),
            pltpu.VMEM((m * most, HD), F32),
            pltpu.VMEM((slots, plen, 2 * HD), BF16),
        ]
        + [pltpu.VMEM((pool, packed, 2 * HD), BF16) for _ in range(heads)]
        + [
            dma((2,)),
            dma((n, heads, PIECES)),
            dma((2, n, heads, PIECES)),
            dma((pool // 2, heads, PIECES)),
            dma((pool, heads, PIECES)),
            dma((pool // 2, heads, PIECES)),
        ],
        compiler_params=pltpu.CompilerParams(
            collective_id=0, has_side_effects=True, vmem_limit_bytes=60 << 20
        ),
    )(
        prompt_states, kv_weight, target, ptab, query_old, step_old, old_cache, tab_old,
        query_new, step_new, tab_new, old_lens[0], off_new, len_new,
    )


def solution(mesh):
    both = ("rep", "pool")
    return jax.shard_map(
        local,
        mesh=mesh,
        in_specs=(
            P(both, "tp"),
            P("tp", None),
            P(both, None),
            P(both, None),
            P(both, None, "tp"),
            P(both, None),
            P(None, both, "tp"),
            P(None, both, "tp"),
            P(None, both, "tp"),
            P(None, both, "tp"),
        ),
        out_specs=(P(None, both, "tp"), P(None, both, "tp")),
        check_vma=False,
    )
```

time: 253 us -> 183 us (0.72)
  Pallas kernels: 0 us -> 163 us
  waiting for transfers between devices: 133 us -> 0 us
  matrix products: 50.2 us -> 0 us
  local copies, waits for them, and re-layouts: 38.6 us -> 5.43 us
  between operations: 15.1 us -> 0.68 us
    pallas_call x0 -> x1, Pallas kernels: none -> 163 us  [local(): pl.pallas_call(functools.partial(kernel, dims), out_shape=(jax.ShapeDtype...]
    reduce_scatter x1 -> x0, waiting for transfers between devices: 110 us -> none  [local(): lax.psum_scatter(lax.dot_general(kv_weight, prompt_states, (((0,), (1,)),...]
    dot_general x10 -> x0, matrix products: 50.2 us -> none  [the longest x1 33.9 us: local(): lax.dot_general(kv_weight, prompt_states, (((0,), (1,)), ((), ())), prefe...]
    all_gather x1 -> x0, waiting for transfers between devices: 22.9 us -> none  [local(): p_cache = lax.all_gather(flat_cache, 'pool', axis=0, tiled=True)]
    slice x6 -> x1, local copies, waits for them, and re-layouts: 13.8 us -> 0.01 us  [local(): all_lens, dest = (meta[:, 0], meta[:, 1])]
    unnamed x41 -> x6, local copies, waits for them, and re-layouts: 13.1 us -> 4.54 us
    reshape x4 -> x1, local copies, waits for them, and re-layouts: 8.08 us -> 0.61 us  [local(): jnp.sum(jnp.where(hit, all_begin[:, None], 0), axis=2).reshape(slots)]
    all_gather x0 -> x1, blocking collectives: none -> 5.06 us  [local(): meta = lax.all_gather(jnp.stack([lens, placement[:, 0]]), 'pool')]
  transfers between devices with their start and end apart: 2 -> 0, of which waited for: 2 -> 0; matrix products, arithmetic and copies ran while one was open for 12% -> 0% of each run, Pallas kernels for 0% -> 0%
where the time goes in v1:
time: 183 us; the launch traced here: 181 us
  Pallas kernels  163 us (89%)
  other arithmetic  7.27 us (4%)
  local copies, waits for them, and re-layouts  5.43 us (3%)
  blocking collectives  5.06 us (3%)
    pallas_call x1, Pallas kernels, local(): pl.pallas_call(functools.partial(kernel, dims), out_shape=(jax.ShapeDtype...  163 us
    all_gather x1, blocking collectives, local(): meta = lax.all_gather(jnp.stack([lens, placement[:, 0]]), 'pool')  5.06 us
    unnamed x6, local copies, waits for them, and re-layouts  4.54 us

profile of v1, /device:TPU:12, one launch (start us, length us, event | category | flops | bytes accessed | tf_op | source)
XLA Modules:
  0.0 181.2 jit_solution(15562558576723655815)
XLA Ops:
  0.6 0.8 reduce-window.8
  1.5 0.7 bitcast_subtract_fusion
  2.1 0.7 add_bitcast_fusion
  2.8 0.7 add_convert_fusion.1
  3.5 5.1 %all-gather.1 = s32[4,2,12]{2,1,0:T(2,128)S(1)} all-gather(s32[1,2,12]{2,1,0:T(2,128)S(1)} %add_bitcast_fusion), channel_id=2, replica_groups=mesh['rep'=2,'pool'=4,'tp'=4] {'pool'}, dimensions={0}, use_global_device_ids=true | all-gather | bytes 480 | tf_op jit(solution)/shard_map/all_gather | solution.py:378
  8.5 0.7 reduce_window_sum.25
  9.3 0.7 reduce_window_sum.24
  10.0 0.3 select_reduce_fusion
  10.3 0.1 copy.14
  10.4 0.6 reshape.148.off_new
  11.0 0.1 copy.13
  11.1 0.1 add.63.len_new
  11.2 0.0 copy-start
  11.2 0.7 select_bitcast_fusion
  12.0 0.6 copy.19
  12.6 0.2 multiply_cosine_fusion.1
  12.8 0.7 pad_maximum_fusion.1.tab_old
  13.5 0.3 multiply_cosine_fusion
  13.7 0.8 pad_maximum_fusion.tab_new
  14.5 0.0 copy-done
  14.5 162.8 %shard_map.122 = (bf16[4,16,4096]{2,1,0:T(8,128)(2,1)}, bf16[4,24,4096]{2,1,0:T(8,128)(2,1)}) custom-call(bf16[1536,4096]{1,0:T(8,128)(2,1)} %x.1, bf16[4096,2048]{1,0:T(8,128)(2,1)} %w.1, s32[1,1536]{1,0:T(1,128)} %bitcast.21, f32[128,256]{1,0:T(8,128)} %constant.26.clone.ptab, bf16[4,16,4096]{2,1,0:T(8,128)(2,1)} %q_old.1, bf16[4,16,512]{2,1,0:T(8,128)(2,1)} %s_old.1, ...), custom_call_target="tpu_custom_call" | custom-call | tf_op jit(solution)/shard_map/pallas_call | solution.py:405
  177.3 1.9 %copy.23 = bf16[4,16,4096]{2,1,0:T(8,128)(2,1)} copy(bf16[4,16,4096]{2,1,0:T(8,128)(2,1)} %get-tuple-element.14) | data formatting | bytes 1048576
  179.2 2.1 %copy.24 = bf16[4,24,4096]{2,1,0:T(8,128)(2,1)} copy(bf16[4,24,4096]{2,1,0:T(8,128)(2,1)} %get-tuple-element.15) | data formatting | bytes 1572864
  (7 shorter events, 0.0 us)
Async XLA Ops:
  11.2 3.3 %copy-start = (s32[24]{0:T(128)}, s32[24]{0:T(128)S(1)}, u32[]{:S(2)}) copy-start(s32[24]{0:T(128)S(1)} %add.63.len_new) | copy-start | bytes 292

commit v2 on v1

--- a/solution.py
+++ b/solution.py
@@ -179,40 +179,36 @@
                 ).astype(BF16)
                 down(low, h, p).start()
 
-            last = jnp.maximum(
-                jnp.where(z > 0, n - 1 - z, 0), jnp.where(z < n - 1, z, 0)
-            )
-
-            @pl.when(last == s)
-            def _():
-                mine = pbuf[h].at[me, span(p)]
-
-                @pl.when(z == 0)
-                def _():
-                    down(z, h, p).wait_recv()
-                    mine[...] = (
-                        part[z, h, span(p)].astype(F32) + rbuf[1, z, h, span(p)].astype(F32)
-                    ).astype(BF16)
-
-                @pl.when(z == n - 1)
-                def _():
-                    up(z, h, p).wait_recv()
-                    mine[...] = (
-                        part[z, h, span(p)].astype(F32) + rbuf[0, z, h, span(p)].astype(F32)
-                    ).astype(BF16)
-
-                @pl.when((z > 0) & (z < n - 1))
-                def _():
-                    up(z, h, p).wait_recv()
-                    down(z, h, p).wait_recv()
-                    mine[...] = (
-                        part[z, h, span(p)].astype(F32)
-                        + rbuf[0, z, h, span(p)].astype(F32)
-                        + rbuf[1, z, h, span(p)].astype(F32)
-                    ).astype(BF16)
-
-                for k in range(chips):
-                    share(h, p, k).start()
+    def finish(h):
+        for p in range(PIECES):
+            mine = pbuf[h].at[me, span(p)]
+
+            @pl.when(z == 0)
+            def _():
+                down(z, h, p).wait_recv()
+                mine[...] = (
+                    part[z, h, span(p)].astype(F32) + rbuf[1, z, h, span(p)].astype(F32)
+                ).astype(BF16)
+
+            @pl.when(z == n - 1)
+            def _():
+                up(z, h, p).wait_recv()
+                mine[...] = (
+                    part[z, h, span(p)].astype(F32) + rbuf[0, z, h, span(p)].astype(F32)
+                ).astype(BF16)
+
+            @pl.when((z > 0) & (z < n - 1))
+            def _():
+                up(z, h, p).wait_recv()
+                down(z, h, p).wait_recv()
+                mine[...] = (
+                    part[z, h, span(p)].astype(F32)
+                    + rbuf[0, z, h, span(p)].astype(F32)
+                    + rbuf[1, z, h, span(p)].astype(F32)
+                ).astype(BF16)
+
+            for k in range(chips):
+                share(h, p, k).start()
 
     def spread(h):
         for p in range(PIECES):
@@ -258,9 +254,9 @@
                 keep = ((col >= low) & (col < high)) | recent
                 score = jnp.where(keep, score, -1e30)
                 top = jnp.max(score, axis=-1, keepdims=True)
-                e = jnp.where(keep, jnp.exp(score - top), 0.0)
+                e = jnp.exp(score - top)
                 total = jnp.sum(e, axis=-1, keepdims=True)
-                got = jnp.dot((e / total).astype(BF16), values, preferred_element_type=F32)
+                got = jnp.dot(e.astype(BF16), values, preferred_element_type=F32) / total
                 os_[pl.ds(b, m, stride=count), :] = got
             return carry
 
@@ -299,35 +295,44 @@
         lax.fori_loop(0, pool, body, 0)
 
     def old(h):
-        attend(h, q_old, s_old, tab_old, o_old, resident, cache.shape[1], 4, q_old.shape[1])
+        attend(h, q_old, s_old, tab_old, o_old, resident, cache.shape[1], 8, q_old.shape[1])
 
     def new(h):
         collect(h)
         place(h)
-        attend(h, q_new, s_new, tab_new, o_new, placed, plen, 4, q_new.shape[1])
-
-    for i in range(n):
-        multiply(i)
-    later = []
-    for h in range(heads):
-        ahead = list(range((h + 1) * n, (h + 2) * n)) if h + 1 < heads else []
-        for s in range(n - 1):
-            relay(h, s)
-            if ahead:
-                multiply(ahead.pop(0))
-            elif later:
-                later.pop(0)()
-        for i in ahead:
+        attend(h, q_new, s_new, tab_new, o_new, placed, plen, 8, q_new.shape[1])
+
+    if heads == 2 and n == 4:
+        for i in range(3):
             multiply(i)
-        spread(h)
-        if h == 0:
-            for g in range(heads):
-                later.append(functools.partial(old, g))
-            if heads > 1:
-                later.pop(0)()
-        later.append(functools.partial(new, h))
-    for f in later:
-        f()
+        relay(0, 0)
+        multiply(3)
+        multiply(4)
+        relay(0, 1)
+        multiply(5)
+        finish(0)
+        multiply(6)
+        relay(1, 0)
+        multiply(7)
+        relay(1, 1)
+        spread(0)
+        old(0)
+        finish(1)
+        old(1)
+        spread(1)
+        new(0)
+        new(1)
+    else:
+        for h in range(heads):
+            for k in range(n):
+                multiply(h * n + k)
+            for at in range(n - 1):
+                relay(h, at)
+            finish(h)
+            spread(h)
+            old(h)
+        for h in range(heads):
+            new(h)
 
     for h in range(heads):
         for p in range(PIECES):
@@ -371,15 +376,16 @@
     cap = slots // pool
 
     lens = prompt_lens[0]
-    begin = jnp.cumsum(lens) - lens
+    before = jnp.arange(prompts)[:, None] > jnp.arange(prompts)[None]
+    begin = jnp.sum(jnp.where(before, lens[None], 0), axis=1)
     k = jnp.arange(plen, dtype=jnp.int32)[None]
     target = jnp.where(k < lens[:, None], begin[:, None] + k, -1).reshape(1, rows)
 
     meta = lax.all_gather(jnp.stack([lens, placement[:, 0]]), "pool")
     all_lens, dest = meta[:, 0], meta[:, 1]
-    all_begin = jnp.cumsum(all_lens, axis=1) - all_lens
+    all_begin = jnp.sum(jnp.where(before[None], all_lens[:, None], 0), axis=2)
     here = (dest == lax.axis_index("pool")).astype(jnp.int32)
-    rank = jnp.cumsum(here, axis=1) - here
+    rank = jnp.sum(jnp.where(before[None], here[:, None], 0), axis=2)
     hit = (here[:, None, :] > 0) & (
         rank[:, None, :] == jnp.arange(cap, dtype=jnp.int32)[None, :, None]
     )

time: 183 us -> 167 us (0.913)
  Pallas kernels: 163 us -> 149 us
    pallas_call x1, Pallas kernels: 163 us -> 149 us  [local(): pl.pallas_call(functools.partial(kernel, dims), out_shape=(jax.ShapeDtype...]
    another operation x3 -> x0, other arithmetic: 2.3 us -> none
where the time goes in v2:
time: 167 us; the launch traced here: 166 us
  Pallas kernels  149 us (89%)
  local copies, waits for them, and re-layouts  5.61 us (3%)
  other arithmetic  5.57 us (3%)
  blocking collectives  5.06 us (3%)
    pallas_call x1, Pallas kernels, local(): pl.pallas_call(functools.partial(kernel, dims), out_shape=(jax.ShapeDtype...  149 us
    all_gather x1, blocking collectives, local(): meta = lax.all_gather(jnp.stack([lens, placement[:, 0]]), 'pool')  5.06 us
    unnamed x6, local copies, waits for them, and re-layouts  4.54 us

profile of v2, /device:TPU:12, one launch (start us, length us, event | category | flops | bytes accessed | tf_op | source)
XLA Modules:
  0.0 166.2 jit_solution(4146191029075351433)
XLA Ops:
  0.6 0.8 select_reduce_fusion.4
  1.4 0.7 add_bitcast_fusion
  2.1 0.7 add_convert_fusion.1
  2.8 5.1 %all-gather.1 = s32[4,2,12]{2,1,0:T(2,128)S(1)} all-gather(s32[1,2,12]{2,1,0:T(2,128)S(1)} %add_bitcast_fusion), channel_id=2, replica_groups=mesh['rep'=2,'pool'=4,'tp'=4] {'pool'}, dimensions={0}, use_global_device_ids=true | all-gather | bytes 480 | tf_op jit(solution)/shard_map/all_gather | solution.py:384
  7.9 0.7 select_bitcast_fusion
  8.6 0.6 copy.21
  9.2 0.5 select_reduce_fusion
  9.7 0.1 copy.15
  9.8 0.1 copy.13
  9.9 0.3 select_reduce_fusion.2
  10.1 0.1 copy.16
  10.2 0.6 reshape.127.off_new
  10.9 0.1 copy.14
  10.9 0.1 add.63.len_new
  11.0 0.0 copy-start
  11.0 0.2 multiply_cosine_fusion.1
  11.2 0.7 pad_maximum_fusion.1.tab_old
  12.0 0.3 multiply_cosine_fusion
  12.2 0.8 pad_maximum_fusion.tab_new
  13.0 0.0 copy-done
  13.0 149.3 %shard_map.122 = (bf16[4,16,4096]{2,1,0:T(8,128)(2,1)}, bf16[4,24,4096]{2,1,0:T(8,128)(2,1)}) custom-call(bf16[1536,4096]{1,0:T(8,128)(2,1)} %x.1, bf16[4096,2048]{1,0:T(8,128)(2,1)} %w.1, s32[1,1536]{1,0:T(1,128)} %bitcast.16, f32[128,256]{1,0:T(8,128)} %constant.19.clone.ptab, bf16[4,16,4096]{2,1,0:T(8,128)(2,1)} %q_old.1, bf16[4,16,512]{2,1,0:T(8,128)(2,1)} %s_old.1, ...), custom_call_target="tpu_custom_call" | custom-call | tf_op jit(solution)/shard_map/pallas_call | solution.py:411
  162.3 1.9 %copy.25 = bf16[4,16,4096]{2,1,0:T(8,128)(2,1)} copy(bf16[4,16,4096]{2,1,0:T(8,128)(2,1)} %get-tuple-element.16) | data formatting | bytes 1048576
  164.2 2.1 %copy.26 = bf16[4,24,4096]{2,1,0:T(8,128)(2,1)} copy(bf16[4,24,4096]{2,1,0:T(8,128)(2,1)} %get-tuple-element.17) | data formatting | bytes 1572864
  (6 shorter events, 0.0 us)
Async XLA Ops:
  11.0 2.0 %copy-start = (s32[24]{0:T(128)}, s32[24]{0:T(128)S(1)}, u32[]{:S(2)}) copy-start(s32[24]{0:T(128)S(1)} %add.63.len_new) | copy-start | bytes 292
